TPU v7x, 1024 devices: a whole 4x8x16 slice. The times are simulated.
1024 devices in a mesh: ctx: 32 (over y_lo, z), head: 16 (over y_hi, x), dp: 2 (over core).
Axes of the slice: x: 4, y: 8 (y_hi: 4, y_lo: 2; y = y_hi * 2 + y_lo), z: 16, core: 2. Of those that a mesh axis runs over, the one named last changes fastest.
Arguments:
- query: bfloat16 [2, 8192, 16384], P('dp', 'ctx', 'head'), may hold values from -4 to 4
- out_grad: bfloat16 [2, 8192, 16384], P('dp', 'ctx', 'head'), may hold values from -6 to 6
- row_lse: float32 [2, 128, 8192], P('dp', 'head', 'ctx'), may hold values from 6 to 8
- row_delta: float32 [2, 128, 8192], P('dp', 'head', 'ctx'), may hold values from -72 to 72
- key_value: bfloat16 [2, 8192, 4096], P('dp', 'ctx', 'head'), may hold values from -9 to 9
- kv_grad_in: float32 [2, 8192, 4096], P('dp', 'ctx', 'head'), may hold values from -1.8 to 1.8
- layer_input: bfloat16 [2, 8192, 8192], P('dp', 'ctx', 'head'), may hold values from -0.119628906 to 0.119628906
- slot_order: int32 [64], replicated, may hold values from 0 to 63, each once
Outputs:
- q_grad: float32 [2, 8192, 16384], P('dp', 'ctx', 'head')
- kv_grad: float32 [2, 8192, 4096], P('dp', 'ctx', 'head')
- v_weight_grad: float32 [16, 512, 2048], P('head', ('ctx', 'dp'))
Inputs may be any that keep to these rules, and one draw needn't show every extreme that they name: `slot_order`: A permutation of the slots: every part of 128 tokens of the sequence sits in exactly one slot; device i of ctx holds slots 2i and 2i+1.
All inputs are finite; a program needn't handle non-finite values.
Results may differ from a plain program's by a relative error of at most 0.0037.
Values may be sent and summed in bfloat16 or wider, within the bound.
A program may use at most 32 MiB of HBM per device.

v0:
```python
import math

import jax
import jax.numpy as jnp
from jax import lax
from jax.sharding import PartitionSpec as P


def from_behind(value, axis, steps):
    count = lax.axis_size(axis)
    pairs = [(source, (source + steps) % count) for source in range(count)]
    return lax.ppermute(value, axis, pairs)


def block_positions(slot_pairs, block_idx, half_len):
    chosen = (jnp.arange(slot_pairs.shape[0], dtype=jnp.int32) == block_idx).astype(jnp.int32)
    starts = jnp.sum(slot_pairs * chosen[:, None], axis=0)
    return (starts[:, None] * half_len + jnp.arange(half_len, dtype=jnp.int32)[None, :]).reshape(-1)


def fetch_block(kv_rows, offset):
    return from_behind(kv_rows, "ctx", offset)


def give_back(partial_rows, offset):
    return from_behind(partial_rows, "ctx", offset)


def pair_grads(
    query_blk, dout_blk, lse_blk, delta_blk, key_rows, value_rows, query_pos, key_pos, softmax_scale
):
    scores = (
        jnp.einsum("qhd,kd->hqk", query_blk, key_rows, preferred_element_type=jnp.float32)
        * softmax_scale
    )
    visible = key_pos[None, None, :] <= query_pos[None, :, None]
    weights = jnp.exp(jnp.where(visible, scores - lse_blk[:, :, None], -1e30))
    weights_low = weights.astype(jnp.bfloat16)
    value_dots = jnp.einsum("qhd,kd->hqk", dout_blk, value_rows, preferred_element_type=jnp.float32)
    score_grad = (weights * (value_dots - delta_blk[:, :, None])).astype(jnp.bfloat16)
    query_grad = (
        jnp.einsum("hqk,kd->qhd", score_grad, key_rows, preferred_element_type=jnp.float32)
        * softmax_scale
    )
    key_grad = (
        jnp.einsum("hqk,qhd->kd", score_grad, query_blk, preferred_element_type=jnp.float32)
        * softmax_scale
    )
    value_part = jnp.einsum(
        "hqk,qhd->kd", weights_low, dout_blk, preferred_element_type=jnp.float32
    )
    return (query_grad, key_grad, value_part)


def on_device(query, out_grad, row_lse, row_delta, key_value, kv_grad_in, layer_input, slot_order):
    cycle_size = lax.axis_size("ctx")
    cycle_index = lax.axis_index("ctx")
    block_len = query.shape[1]
    half_len = block_len // 2
    head_dim = key_value.shape[2] // 2
    heads_here = query.shape[2] // head_dim
    softmax_scale = 1.0 / math.sqrt(head_dim)
    slot_pairs = slot_order.reshape(cycle_size, 2)
    query_pos = block_positions(slot_pairs, cycle_index, half_len)
    key_pos = jnp.concatenate(
        [
            block_positions(slot_pairs, (cycle_index + cycle_size - 1) % cycle_size, half_len),
            block_positions(slot_pairs, (cycle_index + 1) % cycle_size, half_len),
        ],
        axis=0,
    )
    kv_local = key_value[0]
    from_left = fetch_block(kv_local, 1)
    from_right = fetch_block(kv_local, -1)
    kv_both = jnp.concatenate([from_left, from_right], axis=0)
    key_rows = kv_both[:, :head_dim]
    value_rows = kv_both[:, head_dim:]
    query_rows = query[0].reshape(block_len, heads_here, head_dim)
    dout_rows = out_grad[0].reshape(block_len, heads_here, head_dim)
    lse_rows = row_lse[0]
    delta_rows = row_delta[0]
    block_rows = min(block_len, 512)
    block_count = block_len // block_rows

    def advance(running, block_idx):
        query_grad, key_grad, value_part = pair_grads(
            query_rows,
            dout_rows,
            lse_rows,
            delta_rows,
            key_rows,
            value_rows,
            query_pos,
            key_pos,
            softmax_scale,
        )
        return ((running[0] + key_grad, running[1] + value_part), query_grad)

    zero_rows = jnp.zeros((2 * block_len, head_dim), jnp.float32)
    (key_grad, value_part), query_blocks = lax.scan(
        advance, (zero_rows, zero_rows), jnp.arange(block_count, dtype=jnp.int32)
    )
    q_grad = query_blocks.reshape(block_len, heads_here * head_dim)[None]
    partial_rows = jnp.concatenate([key_grad, value_part], axis=1)
    back_from_right = give_back(partial_rows[:block_len], -1)
    back_from_left = give_back(partial_rows[block_len:], 1)
    kv_grad = kv_grad_in[0] + back_from_right + back_from_left
    value_grad = kv_grad[:, head_dim:].astype(jnp.bfloat16)
    features = layer_input[0]
    weight_term = lax.dot_general(
        features,
        lax.all_gather(value_grad, "head", axis=1, tiled=True),
        (((0,), (0,)), ((), ())),
        preferred_element_type=jnp.float32,
    )
    weight_rows = lax.psum_scatter(weight_term, ("ctx", "dp"), scatter_dimension=0, tiled=True)
    return (q_grad, kv_grad[None], weight_rows[None])


def solution(mesh):
    in_specs = (
        P("dp", "ctx", "head"),
        P("dp", "ctx", "head"),
        P("dp", "head", "ctx"),
        P("dp", "head", "ctx"),
        P("dp", "ctx", "head"),
        P("dp", "ctx", "head"),
        P("dp", "ctx", "head"),
        P(),
    )
    out_specs = (P("dp", "ctx", "head"), P("dp", "ctx", "head"), P("head", ("ctx", "dp"), None))
    return jax.shard_map(
        on_device, mesh=mesh, in_specs=in_specs, out_specs=out_specs, check_vma=False
    )
```

profile of v0, /device:TPU:1, one launch (start us, length us, event | category | flops | bytes accessed | tf_op | source)
XLA Modules:
  0.0 364.8 jit_solution(595340045837776911)
XLA Ops:
  7.2 19.9 %collective-permute-start.1 = (bf16[256,256]{1,0:T(8,128)(2,1)}, bf16[256,256]{1,0:T(8,128)(2,1)S(1)}, u32[]{:S(2)}, u32[]{:S(2)}) collective-permute-start(bf16[256,256]{1,0:T(8,128)(2,1)} %bitcast.73), channel_id=1, source_target_pairs={{0,992},{32,0},{64,32},{96,64},{128,96},{160,128},{192,160},{224,1... | collective-permute-start | bytes 393224 | tf_op jit(solution)/shard_map/ppermute | solution.py:12
  27.2 1.9 collective-permute-start
  29.2 0.8 reshape.94
  30.4 1.2 copy.54
  31.7 1.2 copy.55
  32.9 2.3 collective-permute-done
  36.0 1.3 fusion.8
  37.3 1.4 fusion.1
  38.7 0.8 fusion.11
  39.5 3.2 collective-permute-start.2
  42.7 2.1 collective-permute-start.3
  44.8 1.1 copy.39
  45.9 1.2 collective-permute-done.2
  47.1 6.0 %collective-permute-done.3 = f32[256,256]{0,1:T(8,128)} collective-permute-done((f32[256,256]{0,1:T(8,128)S(1)}, f32[256,256]{0,1:T(8,128)}, u32[]{:S(2)}, u32[]{:S(2)}) %collective-permute-start.3) | collective-permute-done | bytes 262176 | tf_op jit(solution)/shard_map/ppermute | solution.py:12
  53.1 1.0 fusion.14
  55.6 60.1 %all-gather.2.cloned.1.call-done = bf16[256,2048]{0,1:T(8,128)(2,1)} async-done(((bf16[256,128]{0,1:T(8,128)(2,1)}), bf16[256,2048]{0,1:T(8,128)(2,1)}) %all-gather.2.cloned.1.call-update) | async-done | bytes 1048592 | tf_op jit(solution)/shard_map/all_gather | solution.py:112
  115.7 3.9 %convolution_bitcast_fusion = f32[512,2048]{0,1:T(8,128)} fusion(bf16[256,2048]{0,1:T(8,128)(2,1)} %all-gather.2.cloned.1.call-done, bf16[1,256,512]{2,1,0:T(8,128)(2,1)S(1)} %copy-done), kind=kOutput, calls=%fused_computation.6 | convolution fusion | flops 536870912 | bytes 5505024 | tf_op jit(solution)/shard_map/dot_general | solution.py:110
  119.6 5.4 %copy.52 = f32[512,2048]{1,0:T(8,128)} copy(f32[512,2048]{0,1:T(8,128)} %convolution_bitcast_fusion) | data formatting | bytes 8388608
  125.0 1.4 convolution_multiply_fusion
  126.4 1.3 copy.44
  127.7 1.8 copy.45
  129.5 226.4 %reduce-scatter.4.cloned.1.call-done = f32[8,2048]{1,0:T(8,128)} async-done(((f32[512,2048]{1,0:T(8,128)}), f32[8,2048]{1,0:T(8,128)}) %reduce-scatter.4.cloned.1.call-update) | async-done | bytes 65552
  355.8 1.2 copy.53
  357.0 0.9 copy.46
  (31 shorter events, 2.7 us)
Async XLA Ops:
  7.2 108.5 %copy-start = (bf16[1,256,512]{2,1,0:T(8,128)(2,1)S(1)}, bf16[1,256,512]{2,1,0:T(8,128)(2,1)}, u32[]{:S(2)}) copy-start(bf16[1,256,512]{2,1,0:T(8,128)(2,1)} %param.14) | copy-start | bytes 786436
  7.2 28.8 %copy-start.4 = (f32[1,8,256]{2,1,0:T(8,128)S(1)}, f32[1,8,256]{2,1,0:T(8,128)}, u32[]{:S(2)}) copy-start(f32[1,8,256]{2,1,0:T(8,128)} %param.10) | copy-start | bytes 24580
  7.2 108.5 %all-gather.2.cloned.1.call-start = ((), (), s32[]{:S(2)}) async-start(), calls=%async_computation.1 | async-start | bytes 1114112 | tf_op jit(solution)/shard_map/all_gather | solution.py:112
  7.2 28.0 %collective-permute-start.1 = (bf16[256,256]{1,0:T(8,128)(2,1)}, bf16[256,256]{1,0:T(8,128)(2,1)S(1)}, u32[]{:S(2)}, u32[]{:S(2)}) collective-permute-start(bf16[256,256]{1,0:T(8,128)(2,1)} %bitcast.73), channel_id=1, source_target_pairs={{0,992},{32,0},{64,32},{96,64},{128,96},{160,128},{192,160},{224,1... | collective-permute-start | bytes 393224 | tf_op jit(solution)/shard_map/ppermute | solution.py:12
  27.2 8.0 %collective-permute-start = (bf16[256,256]{1,0:T(8,128)(2,1)}, bf16[256,256]{1,0:T(8,128)(2,1)S(1)}, u32[]{:S(2)}, u32[]{:S(2)}) collective-permute-start(bf16[256,256]{1,0:T(8,128)(2,1)} %bitcast.74), channel_id=1, source_target_pairs={{0,32},{32,64},{64,96},{96,128},{128,160},{160,192},{192,224},{224... | collective-permute-start | bytes 393224 | tf_op jit(solution)/shard_map/ppermute | solution.py:12
  35.2 2.0 copy-start.2
  35.9 1.3 copy-start.3
  39.5 7.6 %collective-permute-start.2 = (f32[256,256]{0,1:T(8,128)S(1)}, f32[256,256]{0,1:T(8,128)S(1)}, u32[]{:S(2)}, u32[]{:S(2)}) collective-permute-start(f32[256,256]{0,1:T(8,128)S(1)} %get-tuple-element.51), channel_id=1, source_target_pairs={{0,992},{32,0},{64,32},{96,64},{128,96},{160,128},{192,160},{224,1... | collective-permute-start | bytes 786440 | tf_op jit(solution)/shard_map/ppermute | solution.py:12
  42.7 10.4 %collective-permute-start.3 = (f32[256,256]{0,1:T(8,128)S(1)}, f32[256,256]{0,1:T(8,128)}, u32[]{:S(2)}, u32[]{:S(2)}) collective-permute-start(f32[256,256]{0,1:T(8,128)S(1)} %get-tuple-element.52), channel_id=1, source_target_pairs={{0,32},{32,64},{64,96},{96,128},{128,160},{160,192},{192,224},{224... | collective-permute-start | bytes 786440 | tf_op jit(solution)/shard_map/ppermute | solution.py:12
  54.1 0.7 copy-start.1
  55.5 300.3 %reduce-scatter.4.cloned.1.call-start = ((), (), s32[]{:S(2)}) async-start(), calls=%async_computation.2 | async-start | bytes 4259840
Sparse Core Ops, SparseCore 0:
  55.6 59.9 all-gather.1
  125.1 230.6 reduce-scatter.3
where the time goes:
time: 369 us; the launch traced here: 365 us
  waiting for transfers between devices  296 us (80%)
  starting transfers between devices  27.2 us (7%)
  local copies, waits for them, and re-layouts  16.3 us (4%)
  between operations  14.3 us (4%)
  matrix products  9.44 us (3%)
    unnamed x3, waiting for transfers between devices  226 us
    all_gather x1, waiting for transfers between devices, on_device(): lax.all_gather(value_grad, 'head', axis=1, tiled=True)  60.1 us
    ppermute x4, starting transfers between devices, from_behind(): return lax.ppermute(value, axis, pairs)  27.1 us
    unnamed x17, local copies, waits for them, and re-layouts  12.4 us
    ppermute x4, waiting for transfers between devices, from_behind(): return lax.ppermute(value, axis, pairs)  9.5 us
  transfers between devices with their start and end apart: 6, of which 5 were waited for; matrix products, arithmetic and copies ran while one was open for 3% of the time, Pallas kernels for 0%

commit v1 on v0

v1 whole, which is shorter than its diff:
```python
import functools
import math

import jax
import jax.numpy as jnp
from jax import lax
from jax.experimental import pallas as pl
from jax.experimental.pallas import tpu as pltpu
from jax.sharding import PartitionSpec as P

MESH = pl.DeviceIdType.MESH
LOG2E = 1.0 / math.log(2.0)
NYH = 4


def nt(a, b):
    return lax.dot_general(a, b, (((1,), (1,)), ((), ())), preferred_element_type=jnp.float32)


def tn(a, b):
    return lax.dot_general(a, b, (((0,), (0,)), ((), ())), preferred_element_type=jnp.float32)


def nn(a, b):
    return lax.dot_general(a, b, (((1,), (0,)), ((), ())), preferred_element_type=jnp.float32)


def kernel(
    nctx, nx,
    slots, q, do, lse, delta, kv, kvin, feats,
    qg, kvg, wg,
    kb, vb, prob, dv, dk, rdv, rdk, lt, vgb, vall, acc, rp, rm, fin, gat, lrow,
    s_kv, r_kv, s_part, r_part, s_l, r_l, r_core, s_v, r_v, s_p, r_p, s_m, r_m, s_f, r_f,
):
    ctx, head, p = lax.axis_index("ctx"), lax.axis_index("head"), lax.axis_index("dp")
    nz = nctx // 2
    np_, nm = nz // 2, nz - 1 - nz // 2
    e, z = ctx // nz, ctx % nz
    yh, x = head // nx, head % nx
    S, dh = kb.shape[1], kb.shape[2]
    half = S // 2
    hq = q.shape[1] // dh
    F = feats.shape[1]
    scale = 1.0 / math.sqrt(dh)
    left, right = (ctx + nctx - 1) % nctx, (ctx + 1) % nctx
    mine = 2 * e + p
    xs = [(x + r) % nx for r in range(nx)]

    def dev(c=ctx, h=head, d=p):
        return (c, h, d)

    def at(e_=e, z_=z, y_=yh, x_=x, p_=p):
        return (e_ * nz + z_, y_ * nx + x_, p_)

    def send(src, dst, ss, rs, to):
        copy = pltpu.make_async_remote_copy(
            src_ref=src, dst_ref=dst, send_sem=ss, recv_sem=rs, device_id=to, device_id_type=MESH
        )
        copy.start()
        return copy

    def arrived(dst, rs):
        pltpu.make_async_remote_copy(
            src_ref=dst, dst_ref=dst, send_sem=rs, recv_sem=rs, device_id=dev(d=1 - p), device_id_type=MESH
        ).wait_recv()

    barrier = pltpu.get_barrier_semaphore()

    def greet(to):
        pl.semaphore_signal(barrier, inc=1, device_id=to, device_id_type=MESH)

    greet(dev(c=left))
    greet(dev(c=right))
    greet(at(z_=(z + 1) % nz))
    greet(at(z_=(z + nz - 1) % nz))
    group = [(r, a, b) for r in range(nx) for a in (0, 1) for b in (0, 1) if (r, a, b) != (0, 0, 0)]

    def member(r, a, b):
        return (1 - e if a else e), xs[r], (1 - p if b else p)

    for r, a, b in group:
        e_, x_, p_ = member(r, a, b)
        greet(at(e_=e_, x_=x_, p_=p_))

    @pl.when(mine != yh)
    def _():
        for e_ in (0, 1):
            for p_ in (0, 1):
                greet(at(e_=e_, y_=mine, p_=p_))

    pl.semaphore_wait(barrier, 4 + len(group) + NYH - 1)

    sends = []
    for part, buf in ((0, kb), (1, vb)):
        cols = slice(part * dh, (part + 1) * dh)
        for side, to in ((0, right), (1, left)):
            sends.append(send(kv.at[:, cols], buf.at[side], s_kv.at[part, side], r_kv.at[part, side], dev(c=to)))

    lt[x, e, p] = feats[...].T
    own = lt.at[x, e, p]
    sends.append(send(own, own, s_l.at[0], r_l.at[0], at(e_=1 - e)))
    if nx > 1:
        xp, xm, xo = xs[1], xs[nx - 1], xs[2]
        sends.append(send(own, own, s_l.at[1], r_l.at[1], at(x_=xp)))
        sends.append(send(own, own, s_l.at[2], r_l.at[3], at(x_=xm)))
    sends.append(send(own, own, s_l.at[3], r_core.at[0], at(p_=1 - p)))

    for side, blk in ((0, left), (1, right)):
        for kh in (0, 1):
            for qh in (0, 1):
                hidden = jnp.where(slots[2 * blk + kh] < slots[2 * ctx + qh], 0.0, 1e30).astype(jnp.float32)
                lanes = slice(qh * half, (qh + 1) * half)
                lrow[side, kh, :, lanes] = lse[:, lanes] * LOG2E + hidden

    for side, to in ((0, left), (1, right)):
        arrived(kb.at[side], r_kv.at[0, side])
        dv[side] = jnp.zeros((S, dh), jnp.float32)

        def value_step(m, carry, side=side):
            lanes = pl.ds(pl.multiple_of(m * dh, dh), dh)
            st = nt(kb[side], q[:, lanes]) * (scale * LOG2E)
            st = st.reshape(2, half, S) - lrow[side, :, pl.ds(m, 1), :]
            pr = jnp.exp2(st).reshape(S, S)
            prob[m, side] = pr
            dv[side] += nn(pr.astype(jnp.bfloat16), do[:, lanes])
            return carry

        lax.fori_loop(0, hq, value_step, 0)
        sends.append(send(dv.at[side], rdv.at[side], s_part.at[0, side], r_part.at[0, side], dev(c=to)))

    dk[...] = jnp.zeros(dk.shape, jnp.float32)
    for side in (0, 1):
        arrived(vb.at[side], r_kv.at[1, side])

    def rest_step(m, carry):
        lanes = pl.ds(pl.multiple_of(m * dh, dh), dh)
        qm, dom = q[:, lanes], do[:, lanes]
        total = None
        for side in (0, 1):
            dots = nt(vb[side], dom) - delta[pl.ds(m, 1), :]
            ds = (prob[m, side] * dots).astype(jnp.bfloat16)
            dk[side] += nn(ds, qm)
            term = tn(ds, kb[side])
            total = term if total is None else total + term
        qg[:, lanes] = total * scale
        return carry

    lax.fori_loop(0, hq, rest_step, 0)
    for side, to in ((0, left), (1, right)):
        dk[side] = dk[side] * scale
        sends.append(send(dk.at[side], rdk.at[side], s_part.at[1, side], r_part.at[1, side], dev(c=to)))

    for side in (0, 1):
        arrived(rdv.at[side], r_part.at[0, side])
    new_v = kvin[:, dh:] + rdv[0] + rdv[1]
    kvg[:, dh:] = new_v
    vgb[...] = new_v.astype(jnp.bfloat16)
    te, tp = yh // 2, yh % 2
    for o in range(1, NYH):
        sends.append(send(vgb, vall.at[e, p], s_v.at[o], r_v.at[e, p], at(e_=te, y_=(yh + o) % NYH, p_=tp)))

    @pl.when(mine == yh)
    def _():
        vall[e, p] = vgb[...]

    @pl.when(mine != yh)
    def _():
        send(vgb, vall.at[e, p], s_v.at[0], r_v.at[e, p], at(e_=te, p_=tp))

    n_l = 4
    core = 1

    def pass_on(ref, sem, to):
        nonlocal n_l
        sends.append(send(ref, ref, s_l.at[n_l], sem, to))
        n_l += 1

    other = lt.at[x, 1 - e, p]
    arrived(other, r_l.at[0])
    if nx > 1:
        pass_on(other, r_l.at[2], at(x_=xp))
        pass_on(other, r_l.at[4], at(x_=xm))
    pass_on(other, r_core.at[1], at(p_=1 - p))
    hf = F // 2
    if nx > 1:
        for a in (0, 1):
            e_ = 1 - e if a else e
            low = lt.at[xm, e_, p]
            arrived(low, r_l.at[1 + a])
            pass_on(low.at[:hf], r_l.at[5 + a], at(x_=xp))
            pass_on(low, r_core.at[2 + a], at(p_=1 - p))
            high = lt.at[xp, e_, p]
            arrived(high, r_l.at[3 + a])
            pass_on(high.at[hf:], r_l.at[7 + a], at(x_=xm))
            pass_on(high, r_core.at[4 + a], at(p_=1 - p))

    for side in (0, 1):
        arrived(rdk.at[side], r_part.at[1, side])
    kvg[:, :dh] = kvin[:, :dh] + rdk[0] + rdk[1]

    for e_ in (0, 1):
        for p_ in (0, 1):
            @pl.when((mine != yh) | (e_ != e) | (p_ != p))
            def _(e_=e_, p_=p_):
                arrived(vall.at[e_, p_], r_v.at[e_, p_])

    zp, zm = at(z_=(z + 1) % nz), at(z_=(z + nz - 1) % nz)

    def up(step, r, src):
        return send(src, rp.at[step, r], s_p.at[step, r], r_p.at[step, r], zp)

    def down(step, r, src):
        return send(src, rm.at[step, r], s_m.at[step, r], r_m.at[step, r], zm)

    def weight_term(r, sems):
        for i in sems:
            k, a = i
            e_ = 1 - e if a else e
            arrived(lt.at[xs[r], e_, 1 - p], r_core.at[k])
        total = None
        for e_ in (0, 1):
            for p_ in (0, 1):
                term = nn(lt[xs[r], e_, p_], vall[e_, p_])
                total = term if total is None else total + term
        acc[r] = total.reshape(acc.shape[1:])
        up(0, r, acc.at[r, :, (z + np_) % nz])
        if nm:
            down(0, r, acc.at[r, :, (z + nz - nm) % nz])

    weight_term(0, ((0, 0), (1, 1)))
    if nx > 1:
        weight_term(nx - 1, ((2, 0), (3, 1)))
        weight_term(1, ((4, 0), (5, 1)))
        for a in (0, 1):
            e_ = 1 - e if a else e
            far = lt.at[xo, e_, p]
            arrived(far.at[:hf], r_l.at[5 + a])
            arrived(far.at[hf:], r_l.at[7 + a])
            pass_on(far, r_core.at[6 + a], at(p_=1 - p))
        weight_term(2, ((6, 0), (7, 1)))
    order = (0, nx - 1, 1, 2) if nx > 1 else (0,)

    def chain(step, both):
        for r in order:
            arrived(rp.at[step, r], r_p.at[step, r])
            rp[step, r] += acc[r, :, (z + np_ - 1 - step) % nz]
            up(step + 1, r, rp.at[step, r])
            if both:
                arrived(rm.at[step, r], r_m.at[step, r])
                rm[step, r] += acc[r, :, (z + nz - nm + 1 + step) % nz]
                down(step + 1, r, rm.at[step, r])

    def chain_step(step, carry):
        chain(step, True)
        return carry

    if nm > 1:
        lax.fori_loop(0, nm - 1, chain_step, 0)
    for step in range(max(nm - 1, 0), np_ - 1):
        chain(step, False)

    for r in order:
        whole = acc[r, :, z]
        arrived(rp.at[np_ - 1, r], r_p.at[np_ - 1, r])
        whole = whole + rp[np_ - 1, r]
        if nm:
            arrived(rm.at[nm - 1, r], r_m.at[nm - 1, r])
            whole = whole + rm[nm - 1, r]
        fin[r] = whole.reshape(fin.shape[1:])
        for i, (r_, a, b) in enumerate(group):
            if r_ == r:
                e_, x_, p_ = member(r, a, b)
                col = mine * nx + x
                sends.append(
                    send(fin.at[r, e_, p_], gat.at[col], s_f.at[i], r_f.at[r, a, b], at(e_=e_, x_=x_, p_=p_))
                )
    gat[mine * nx + x] = fin[0, e, p]
    for r, a, b in group:
        e_, _, p_ = member(r, a, b)
        col = (2 * e_ + p_) * nx + xs[(nx - r) % nx]
        arrived(gat.at[col], r_f.at[r, a, b])
    for c in range(NYH * nx):
        wg[:, c * dh : (c + 1) * dh] = gat[c]

    for copy in sends:
        copy.wait_send()

    @pl.when(mine != yh)
    def _():
        pltpu.make_async_remote_copy(
            src_ref=vgb, dst_ref=vall.at[e, p], send_sem=s_v.at[0], recv_sem=r_v.at[e, p],
            device_id=at(e_=te, p_=tp), device_id_type=MESH,
        ).wait_send()

    def left_(src, ss):
        pltpu.make_async_remote_copy(
            src_ref=src, dst_ref=src, send_sem=ss, recv_sem=ss, device_id=zp, device_id_type=MESH
        ).wait_send()

    for r in order:
        left_(acc.at[r, :, 0], s_p.at[0, r])
        if nm:
            left_(acc.at[r, :, 0], s_m.at[0, r])

    def drain(step, carry):
        for r in order:
            left_(rp.at[0, r], s_p.at[step, r])
        return carry

    def drain_m(step, carry):
        for r in order:
            left_(rm.at[0, r], s_m.at[step, r])
        return carry

    lax.fori_loop(1, np_, drain, 0)
    if nm > 1:
        lax.fori_loop(1, nm, drain_m, 0)


def on_device(nctx, nx, query, out_grad, row_lse, row_delta, key_value, kv_grad_in, layer_input, slot_order):
    S, dh = query.shape[1], key_value.shape[2] // 2
    hq = query.shape[2] // dh
    F = layer_input.shape[2]
    nz = nctx // 2
    rows = F // (2 * nctx)
    np_, nm = nz // 2, max(nz - 1 - nz // 2, 1)
    f32, bf16 = jnp.float32, jnp.bfloat16
    vmem = pl.BlockSpec(memory_space=pltpu.VMEM)
    dma = pltpu.SemaphoreType.DMA
    piece = (nx, 2, 2 * rows, dh)
    outs = pl.pallas_call(
        functools.partial(kernel, nctx, nx),
        out_shape=(
            jax.ShapeDtypeStruct((S, hq * dh), f32),
            jax.ShapeDtypeStruct((S, 2 * dh), f32),
            jax.ShapeDtypeStruct((rows, NYH * nx * dh), f32),
        ),
        in_specs=[pl.BlockSpec(memory_space=pltpu.SMEM)] + [vmem] * 7,
        out_specs=(vmem,) * 3,
        scratch_shapes=[
            pltpu.VMEM((2, S, dh), bf16),
            pltpu.VMEM((2, S, dh), bf16),
            pltpu.VMEM((hq, 2, S, S), f32),
            pltpu.VMEM((2, S, dh), f32),
            pltpu.VMEM((2, S, dh), f32),
            pltpu.VMEM((2, S, dh), f32),
            pltpu.VMEM((2, S, dh), f32),
            pltpu.VMEM((nx, 2, 2, F, S), bf16),
            pltpu.VMEM((S, dh), bf16),
            pltpu.VMEM((2, 2, S, dh), bf16),
            pltpu.VMEM((nx, 2, nz, 2 * rows, dh), f32),
            pltpu.VMEM((np_,) + piece, f32),
            pltpu.VMEM((nm,) + piece, f32),
            pltpu.VMEM((nx, 2, 2, rows, dh), f32),
            pltpu.VMEM((NYH * nx, rows, dh), f32),
            pltpu.VMEM((2, 2, hq, S), f32),
            dma((2, 2)), dma((2, 2)), dma((2, 2)), dma((2, 2)),
            dma((20,)), dma((9,)), dma((8,)),
            dma((4,)), dma((2, 2)),
            dma((np_, nx)), dma((np_, nx)), dma((nm, nx)), dma((nm, nx)),
            dma((16,)), dma((nx, 2, 2)),
        ],
        compiler_params=pltpu.CompilerParams(
            collective_id=0, has_side_effects=True, vmem_limit_bytes=48 * 1024 * 1024
        ),
        cost_estimate=pl.CostEstimate(flops=2_000_000_000, bytes_accessed=6_000_000, transcendentals=1_000_000),
    )(
        slot_order, query[0], out_grad[0], row_lse[0], row_delta[0], key_value[0], kv_grad_in[0], layer_input[0]
    )
    return outs[0][None], outs[1][None], outs[2][None]


def solution(mesh):
    nctx, nhead = mesh.shape["ctx"], mesh.shape["head"]
    in_specs = (
        P("dp", "ctx", "head"),
        P("dp", "ctx", "head"),
        P("dp", "head", "ctx"),
        P("dp", "head", "ctx"),
        P("dp", "ctx", "head"),
        P("dp", "ctx", "head"),
        P("dp", "ctx", "head"),
        P(),
    )
    out_specs = (P("dp", "ctx", "head"), P("dp", "ctx", "head"), P("head", ("ctx", "dp"), None))
    return jax.shard_map(
        functools.partial(on_device, nctx, nhead // NYH),
        mesh=mesh, in_specs=in_specs, out_specs=out_specs, check_vma=False,
    )
```

time: 369 us -> 91.3 us (0.25); the launches traced: 365 us -> 90.9 us
  waiting for transfers between devices: 296 us -> 0 us
  Pallas kernels: 0 us -> 81.7 us
  starting transfers between devices: 27.2 us -> 0 us
  between operations: 14.3 us -> 0.67 us
  matrix products: 9.44 us -> 0 us
  local copies, waits for them, and re-layouts: 16.3 us -> 8.57 us
    unnamed x3 -> x0, waiting for transfers between devices: 226 us -> none
    pallas_call x0 -> x1, Pallas kernels: none -> 81.7 us  [on_device(): pl.pallas_call(functools.partial(kernel, nctx, nx), out_shape=(jax.ShapeD...]
    all_gather x1 -> x0, waiting for transfers between devices: 60.1 us -> none  [on_device(): lax.all_gather(value_grad, 'head', axis=1, tiled=True)]
    ppermute x4 -> x0, starting transfers between devices: 27.1 us -> none  [from_behind(): return lax.ppermute(value, axis, pairs)]
    ppermute x4 -> x0, waiting for transfers between devices: 9.5 us -> none  [from_behind(): return lax.ppermute(value, axis, pairs)]
    dot_general x6 -> x0, matrix products: 9.44 us -> none  [the longest x1 3.9 us: on_device(): lax.dot_general(features, lax.all_gather(value_grad, 'head', axis=1, tile...]
    unnamed x17 -> x19, local copies, waits for them, and re-layouts: 12.4 us -> 8.57 us
  transfers between devices with their start and end apart: 6 -> 0, of which waited for: 5 -> 0; matrix products, arithmetic and copies ran while one was open for 3% -> 0% of each run, Pallas kernels for 0% -> 0%
where the time goes in v1:
time: 91.3 us; the launch traced here: 90.9 us
  Pallas kernels  81.7 us (89%)
  local copies, waits for them, and re-layouts  8.57 us (9%)
    pallas_call x1, Pallas kernels, on_device(): pl.pallas_call(functools.partial(kernel, nctx, nx), out_shape=(jax.ShapeD...  81.7 us
    unnamed x19, local copies, waits for them, and re-layouts  8.57 us

profile of v1, /device:TPU:1, one launch (start us, length us, event | category | flops | bytes accessed | tf_op | source)
XLA Modules:
  0.0 90.9 jit_solution(9451266762051348120)
XLA Ops:
  0.6 0.0 copy-start.5
  0.6 0.0 copy-start.7
  0.7 0.7 copy-done.5
  1.3 0.0 copy-done.7
  1.3 0.0 copy-start
  1.3 1.0 %copy-done = bf16[1,256,1024]{2,1,0:T(8,128)(2,1)S(1)} copy-done((bf16[1,256,1024]{2,1,0:T(8,128)(2,1)S(1)}, bf16[1,256,1024]{2,1,0:T(8,128)(2,1)}, u32[]{:S(2)}) %copy-start) | copy-done | bytes 524312
  2.4 0.0 copy-start.1
  2.4 1.0 %copy-done.1 = bf16[1,256,1024]{2,1,0:T(8,128)(2,1)S(1)} copy-done((bf16[1,256,1024]{2,1,0:T(8,128)(2,1)S(1)}, bf16[1,256,1024]{2,1,0:T(8,128)(2,1)}, u32[]{:S(2)}) %copy-start.1) | copy-done | bytes 524312
  3.4 0.0 copy-start.2
  3.4 0.9 %copy-done.2 = f32[1,256,256]{2,1,0:T(8,128)S(1)} copy-done((f32[1,256,256]{2,1,0:T(8,128)S(1)}, f32[1,256,256]{2,1,0:T(8,128)}, u32[]{:S(2)}) %copy-start.2) | copy-done | bytes 262168
  4.4 0.0 copy-start.3
  4.4 0.9 %copy-done.3 = bf16[1,256,512]{2,1,0:T(8,128)(2,1)S(1)} copy-done((bf16[1,256,512]{2,1,0:T(8,128)(2,1)S(1)}, bf16[1,256,512]{2,1,0:T(8,128)(2,1)}, u32[]{:S(2)}) %copy-start.3) | copy-done | bytes 262168
  5.3 0.0 copy-start.4
  5.3 0.9 copy-done.4
  6.2 0.0 copy-start.6
  6.2 0.7 copy-done.6
  6.9 81.7 %shard_map.103 = (f32[256,1024]{1,0:T(8,128)S(1)}, f32[256,256]{1,0:T(8,128)S(1)}, f32[8,2048]{1,0:T(8,128)S(1)}) custom-call(s32[64]{0:T(128)S(1)} %copy-done.7, bf16[256,1024]{1,0:T(8,128)(2,1)S(1)} %bitcast.13, bf16[256,1024]{1,0:T(8,128)(2,1)S(1)} %bitcast.14, f32[8,256]{1,0:T(8,128)S(1)} %bitcast.18, f32[8,256]{1,0:T(8,128)S(1)} %bitcast.19, ...), custom_call_target="tpu_custom_call" | custom-call | flops 2000000000 | bytes 6000000 | tf_op jit(solution)/shard_map/pallas_call | solution.py:331
  88.6 1.0 %copy.14 = f32[1,256,1024]{2,1,0:T(8,128)} copy(f32[1,256,1024]{2,1,0:T(8,128)S(1)} %bitcast.10) | data formatting | bytes 2097152
  89.6 0.7 copy.15
  90.3 0.6 copy.16
Async XLA Ops:
  0.6 0.7 copy-start.5
  0.6 0.7 copy-start.7
  1.3 1.0 %copy-start = (bf16[1,256,1024]{2,1,0:T(8,128)(2,1)S(1)}, bf16[1,256,1024]{2,1,0:T(8,128)(2,1)}, u32[]{:S(2)}) copy-start(bf16[1,256,1024]{2,1,0:T(8,128)(2,1)} %param.8) | copy-start | bytes 1572868
  2.4 1.0 %copy-start.1 = (bf16[1,256,1024]{2,1,0:T(8,128)(2,1)S(1)}, bf16[1,256,1024]{2,1,0:T(8,128)(2,1)}, u32[]{:S(2)}) copy-start(bf16[1,256,1024]{2,1,0:T(8,128)(2,1)} %param.9) | copy-start | bytes 1572868
  3.4 0.9 %copy-start.2 = (f32[1,256,256]{2,1,0:T(8,128)S(1)}, f32[1,256,256]{2,1,0:T(8,128)}, u32[]{:S(2)}) copy-start(f32[1,256,256]{2,1,0:T(8,128)} %param.13) | copy-start | bytes 786436
  4.4 0.9 %copy-start.3 = (bf16[1,256,512]{2,1,0:T(8,128)(2,1)S(1)}, bf16[1,256,512]{2,1,0:T(8,128)(2,1)}, u32[]{:S(2)}) copy-start(bf16[1,256,512]{2,1,0:T(8,128)(2,1)} %param.14) | copy-start | bytes 786436
  5.3 0.9 copy-start.4
  6.2 0.7 copy-start.6

commit v2 on v1

v2 whole, which is shorter than its diff:
```python
import functools
import math

import jax
import jax.numpy as jnp
from jax import lax
from jax.experimental import pallas as pl
from jax.experimental.pallas import tpu as pltpu
from jax.sharding import PartitionSpec as P

MESH = pl.DeviceIdType.MESH
LOG2E = 1.0 / math.log(2.0)
NYH = 4


def nt(a, b):
    return lax.dot_general(a, b, (((1,), (1,)), ((), ())), preferred_element_type=jnp.float32)


def tn(a, b):
    return lax.dot_general(a, b, (((0,), (0,)), ((), ())), preferred_element_type=jnp.float32)


def nn(a, b):
    return lax.dot_general(a, b, (((1,), (0,)), ((), ())), preferred_element_type=jnp.float32)


def kernel(
    nctx, nx,
    slots, q_h, do_h, lse_h, delta_h, kv, kvin_h, feats_h,
    qg, kvg, wg,
    q, do, lse, delta, kvin, feats, kb, vb, prob, dv, dk, rdv, rdk, lt, vgb, vall, acc, odd_out, odd_in, even_out, even_in, fin, gat, lrow,
    s_in, s_kv, r_kv, s_part, r_part, s_l, r_l, r_core, s_v, r_v, s_odd, r_odd, s_even, r_even, s_f, r_f,
):
    ctx, head, p = lax.axis_index("ctx"), lax.axis_index("head"), lax.axis_index("dp")
    nz = nctx // 2
    np_ = nz // 2
    e, z = ctx // nz, ctx % nz
    yh, x = head // nx, head % nx
    S, dh = kb.shape[1], kb.shape[2]
    half = S // 2
    hq = q.shape[1] // dh
    F = feats.shape[1]
    scale = 1.0 / math.sqrt(dh)
    left, right = (ctx + nctx - 1) % nctx, (ctx + 1) % nctx
    mine = 2 * e + p
    xs = [(x + r) % nx for r in range(nx)]

    def dev(c=ctx, h=head, d=p):
        return (c, h, d)

    def at(e_=e, z_=z, y_=yh, x_=x, p_=p):
        return (e_ * nz + z_, y_ * nx + x_, p_)

    def send(src, dst, ss, rs, to):
        copy = pltpu.make_async_remote_copy(
            src_ref=src, dst_ref=dst, send_sem=ss, recv_sem=rs, device_id=to, device_id_type=MESH
        )
        copy.start()
        return copy

    def arrived(dst, rs):
        pltpu.make_async_remote_copy(
            src_ref=dst, dst_ref=dst, send_sem=rs, recv_sem=rs, device_id=dev(d=1 - p), device_id_type=MESH
        ).wait_recv()

    fetched = [
        pltpu.make_async_copy(src, dst, s_in.at[i])
        for i, (src, dst) in enumerate(
            ((feats_h, feats), (lse_h, lse), (q_h, q), (do_h, do), (delta_h, delta), (kvin_h, kvin))
        )
    ]
    for copy in fetched:
        copy.start()

    barrier = pltpu.get_barrier_semaphore()

    def greet(to):
        pl.semaphore_signal(barrier, inc=1, device_id=to, device_id_type=MESH)

    greet(dev(c=left))
    greet(dev(c=right))
    greet(at(z_=(z + 1) % nz))
    greet(at(z_=(z + nz - 1) % nz))
    greet(at(z_=(z + 2) % nz))
    greet(at(z_=(z + nz - 2) % nz))
    group = [(r, a, b) for r in range(nx) for a in (0, 1) for b in (0, 1) if (r, a, b) != (0, 0, 0)]

    def member(r, a, b):
        return (1 - e if a else e), xs[r], (1 - p if b else p)

    for r, a, b in group:
        e_, x_, p_ = member(r, a, b)
        greet(at(e_=e_, x_=x_, p_=p_))

    @pl.when(mine != yh)
    def _():
        for e_ in (0, 1):
            for p_ in (0, 1):
                greet(at(e_=e_, y_=mine, p_=p_))

    pl.semaphore_wait(barrier, 6 + len(group) + NYH - 1)

    sends = []
    for part, buf in ((0, kb), (1, vb)):
        cols = slice(part * dh, (part + 1) * dh)
        for side, to in ((0, right), (1, left)):
            sends.append(send(kv.at[:, cols], buf.at[side], s_kv.at[part, side], r_kv.at[part, side], dev(c=to)))

    fetched[0].wait()
    lt[x, e, p] = feats[...].T
    own = lt.at[x, e, p]
    hf = F // 2
    passed = []

    def pass_on(ref, sem, to):
        passed.append(send(ref, ref, s_l.at[len(passed)], sem, to))

    to_core = at(p_=1 - p)
    pass_on(own, r_l.at[0], at(e_=1 - e))
    if nx > 1:
        xp, xm, xo = xs[1], xs[nx - 1], xs[2]
        pass_on(own, r_l.at[1], at(x_=xp))
        pass_on(own, r_l.at[3], at(x_=xm))
    pass_on(own, r_core.at[0, 0], to_core)

    def share_other():
        other = lt.at[x, 1 - e, p]
        arrived(other, r_l.at[0])
        if nx > 1:
            pass_on(other, r_l.at[2], at(x_=xp))
            pass_on(other, r_l.at[4], at(x_=xm))
        pass_on(other, r_core.at[0, 1], to_core)

    def share_side(a):
        if nx > 1:
            e_ = 1 - e if a else e
            low, high = lt.at[xm, e_, p], lt.at[xp, e_, p]
            arrived(low, r_l.at[1 + a])
            pass_on(low.at[:hf], r_l.at[5 + a], at(x_=xp))
            arrived(high, r_l.at[3 + a])
            pass_on(high.at[hf:], r_l.at[7 + a], at(x_=xm))
            pass_on(low, r_core.at[nx - 1, a], to_core)
            pass_on(high, r_core.at[1, a], to_core)

    def share_far(a):
        if nx > 1:
            far = lt.at[xo, 1 - e if a else e, p]
            arrived(far.at[:hf], r_l.at[5 + a])
            arrived(far.at[hf:], r_l.at[7 + a])
            pass_on(far, r_core.at[2, a], to_core)

    for copy in fetched[1:4]:
        copy.wait()

    for side, blk in ((0, left), (1, right)):
        for kh in (0, 1):
            for qh in (0, 1):
                hidden = jnp.where(slots[2 * blk + kh] < slots[2 * ctx + qh], 0.0, 1e30).astype(jnp.float32)
                lanes = slice(qh * half, (qh + 1) * half)
                lrow[side, kh, :, lanes] = lse[:, lanes] * LOG2E + hidden

    heads = [slice(m * dh, (m + 1) * dh) for m in range(hq)]
    for side, to in ((0, left), (1, right)):
        arrived(kb.at[side], r_kv.at[0, side])
        total = None
        for m, lanes in enumerate(heads):
            st = nt(kb[side], q[:, lanes]) * (scale * LOG2E)
            st = st.reshape(2, half, S) - lrow[side, :, m : m + 1, :]
            pr = jnp.exp2(st).reshape(S, S)
            prob[m, side] = pr
            term = nn(pr.astype(jnp.bfloat16), do[:, lanes])
            total = term if total is None else total + term
        dv[side] = total
        sends.append(send(dv.at[side], rdv.at[side], s_part.at[0, side], r_part.at[0, side], dev(c=to)))

    share_other()

    for copy in fetched[4:]:
        copy.wait()
    for side in (0, 1):
        arrived(vb.at[side], r_kv.at[1, side])
    totals = [None, None]
    for m, lanes in enumerate(heads):
        qm, dom = q[:, lanes], do[:, lanes]
        whole = None
        for side in (0, 1):
            dots = nt(vb[side], dom) - delta[m : m + 1, :]
            ds = (prob[m, side] * dots).astype(jnp.bfloat16)
            term = nn(ds, qm)
            totals[side] = term if totals[side] is None else totals[side] + term
            term = tn(ds, kb[side])
            whole = term if whole is None else whole + term
        qg[:, lanes] = whole
    for side, to in ((0, left), (1, right)):
        dk[side] = totals[side] * scale
        sends.append(send(dk.at[side], rdk.at[side], s_part.at[1, side], r_part.at[1, side], dev(c=to)))

    share_side(0)

    for side in (0, 1):
        arrived(rdv.at[side], r_part.at[0, side])
    new_v = kvin[:, dh:] + rdv[0] + rdv[1]
    kvg[:, dh:] = new_v
    vgb[...] = new_v.astype(jnp.bfloat16)
    te, tp = yh // 2, yh % 2
    for o in range(1, NYH):
        sends.append(send(vgb, vall.at[e, p], s_v.at[o], r_v.at[e, p], at(e_=te, y_=(yh + o) % NYH, p_=tp)))

    @pl.when(mine == yh)
    def _():
        vall[e, p] = vgb[...]

    @pl.when(mine != yh)
    def _():
        send(vgb, vall.at[e, p], s_v.at[0], r_v.at[e, p], at(e_=te, p_=tp))

    share_far(0)
    share_side(1)

    for side in (0, 1):
        arrived(rdk.at[side], r_part.at[1, side])
    kvg[:, :dh] = kvin[:, :dh] + rdk[0] + rdk[1]

    for e_ in (0, 1):
        for p_ in (0, 1):
            @pl.when((mine != yh) | (e_ != e) | (p_ != p))
            def _(e_=e_, p_=p_):
                arrived(vall.at[e_, p_], r_v.at[e_, p_])

    order = (0, nx - 1, 1, 2) if nx > 1 else (0,)
    ng = odd_in.shape[2]
    per = len(order) // ng
    kc = np_ // 2

    def blocks(g):
        return slice(g * per, (g + 1) * per)

    def term_for(g, d, k):
        to = (z + k) % nz if d == 0 else (z + nz - k) % nz
        return acc[blocks(g), :, to]

    def weight_term(i):
        r = order[i]
        for a in (0, 1):
            e_, x_, _ = member(r, a, 0)
            arrived(lt.at[x_, e_, 1 - p], r_core.at[r, a])
        total = None
        for e_ in (0, 1):
            for p_ in (0, 1):
                term = nn(lt[xs[r], e_, p_], vall[e_, p_])
                total = term if total is None else total + term
        acc[i] = total.reshape(acc.shape[1:])

    def next_odd(i, g, d):
        k = np_ - 1 - 2 * i
        odd_out[d, i, g] = term_for(g, d, k).astype(jnp.bfloat16)
        sends.append(send(odd_out.at[d, i, g], odd_in.at[d, i, g], s_odd.at[d, i, g], r_odd.at[d, i, g], beside[d]))

    def stop(i, g, d):
        k = np_ - 2 * i - (0 if d == 0 else 2)
        value = term_for(g, d, k)
        got = i - 1 if d == 0 else i
        if got >= 0:
            arrived(odd_in.at[d, got, g], r_odd.at[d, got, g])
            value = value + odd_in[d, got, g].astype(jnp.float32)
        if i > 0:
            arrived(even_in.at[d, i - 1, g], r_even.at[d, i - 1, g])
            value = value + even_in[d, i - 1, g].astype(jnp.float32)
        even_out[d, i, g] = value.astype(jnp.bfloat16)
        sends.append(
            send(even_out.at[d, i, g], even_in.at[d, i, g], s_even.at[d, i, g], r_even.at[d, i, g], beyond[d])
        )

    beside = (at(z_=(z + 1) % nz), at(z_=(z + nz - 1) % nz))
    beyond = (at(z_=(z + 2) % nz), at(z_=(z + nz - 2) % nz))
    for g in range(ng):
        if per == 2 and g == 1:
            share_far(1)
        for i in range(g * per, (g + 1) * per):
            weight_term(i)
        stop(0, g, 0)
        for i in range(kc):
            next_odd(i, g, 1)
            next_odd(i, g, 0)
    for i in range(kc):
        for g in range(ng):
            if i > 0:
                stop(i, g, 0)
            if i < kc - 1:
                stop(i, g, 1)

    for i, r in enumerate(order):
        g, k = i // per, i % per
        whole = acc[i, :, z]
        for d, n in ((0, kc), (1, kc - 1)):
            if k == 0:
                arrived(odd_in.at[d, kc - 1, g], r_odd.at[d, kc - 1, g])
            whole = whole + odd_in[d, kc - 1, g, k].astype(jnp.float32)
            if n > 0:
                if k == 0:
                    arrived(even_in.at[d, n - 1, g], r_even.at[d, n - 1, g])
                whole = whole + even_in[d, n - 1, g, k].astype(jnp.float32)
        fin[r] = whole.reshape(fin.shape[1:])
        for j, (r_, a, b) in enumerate(group):
            if r_ == r:
                e_, x_, p_ = member(r, a, b)
                col = mine * nx + x
                sends.append(
                    send(fin.at[r, e_, p_], gat.at[col], s_f.at[j], r_f.at[r, a, b], at(e_=e_, x_=x_, p_=p_))
                )
    gat[mine * nx + x] = fin[0, e, p]
    for r, a, b in group:
        e_, _, p_ = member(r, a, b)
        col = (2 * e_ + p_) * nx + xs[(nx - r) % nx]
        arrived(gat.at[col], r_f.at[r, a, b])
    for c in range(NYH * nx):
        wg[:, c * dh : (c + 1) * dh] = gat[c]

    for copy in sends + passed:
        copy.wait_send()

    @pl.when(mine != yh)
    def _():
        pltpu.make_async_remote_copy(
            src_ref=vgb, dst_ref=vall.at[e, p], send_sem=s_v.at[0], recv_sem=r_v.at[e, p],
            device_id=at(e_=te, p_=tp), device_id_type=MESH,
        ).wait_send()


def on_device(nctx, nx, query, out_grad, row_lse, row_delta, key_value, kv_grad_in, layer_input, slot_order):
    S, dh = query.shape[1], key_value.shape[2] // 2
    hq = query.shape[2] // dh
    F = layer_input.shape[2]
    nz = nctx // 2
    rows = F // (2 * nctx)
    kc = nz // 4
    f32, bf16 = jnp.float32, jnp.bfloat16
    vmem = pl.BlockSpec(memory_space=pltpu.VMEM)
    dma = pltpu.SemaphoreType.DMA
    ng = 2 if nx > 1 else 1
    piece = (ng, nx // ng, 2, 2 * rows, dh)
    outs = pl.pallas_call(
        functools.partial(kernel, nctx, nx),
        out_shape=(
            jax.ShapeDtypeStruct((S, hq * dh), f32),
            jax.ShapeDtypeStruct((S, 2 * dh), f32),
            jax.ShapeDtypeStruct((rows, NYH * nx * dh), f32),
        ),
        in_specs=[pl.BlockSpec(memory_space=pltpu.SMEM)] + [pl.BlockSpec(memory_space=pl.ANY)] * 7,
        out_specs=(vmem,) * 3,
        scratch_shapes=[
            pltpu.VMEM((S, hq * dh), bf16),
            pltpu.VMEM((S, hq * dh), bf16),
            pltpu.VMEM((hq, S), f32),
            pltpu.VMEM((hq, S), f32),
            pltpu.VMEM((S, 2 * dh), f32),
            pltpu.VMEM((S, F), bf16),
            pltpu.VMEM((2, S, dh), bf16),
            pltpu.VMEM((2, S, dh), bf16),
            pltpu.VMEM((hq, 2, S, S), f32),
            pltpu.VMEM((2, S, dh), f32),
            pltpu.VMEM((2, S, dh), f32),
            pltpu.VMEM((2, S, dh), f32),
            pltpu.VMEM((2, S, dh), f32),
            pltpu.VMEM((nx, 2, 2, F, S), bf16),
            pltpu.VMEM((S, dh), bf16),
            pltpu.VMEM((2, 2, S, dh), bf16),
            pltpu.VMEM((nx, 2, nz, 2 * rows, dh), f32),
            pltpu.VMEM((2, kc) + piece, bf16),
            pltpu.VMEM((2, kc) + piece, bf16),
            pltpu.VMEM((2, kc) + piece, bf16),
            pltpu.VMEM((2, kc) + piece, bf16),
            pltpu.VMEM((nx, 2, 2, rows, dh), f32),
            pltpu.VMEM((NYH * nx, rows, dh), f32),
            pltpu.VMEM((2, 2, hq, S), f32),
            dma((6,)), dma((2, 2)), dma((2, 2)), dma((2, 2)), dma((2, 2)),
            dma((20,)), dma((9,)), dma((nx, 2)),
            dma((4,)), dma((2, 2)),
            dma((2, kc, ng)), dma((2, kc, ng)), dma((2, kc, ng)), dma((2, kc, ng)),
            dma((16,)), dma((nx, 2, 2)),
        ],
        compiler_params=pltpu.CompilerParams(
            collective_id=0, has_side_effects=True, vmem_limit_bytes=58 * 1024 * 1024
        ),
        cost_estimate=pl.CostEstimate(flops=2_000_000_000, bytes_accessed=6_000_000, transcendentals=1_000_000),
    )(
        slot_order, query[0], out_grad[0], row_lse[0], row_delta[0], key_value[0], kv_grad_in[0], layer_input[0]
    )
    return (outs[0] * (1.0 / math.sqrt(dh)))[None], outs[1][None], outs[2][None]


def solution(mesh):
    nctx, nhead = mesh.shape["ctx"], mesh.shape["head"]
    in_specs = (
        P("dp", "ctx", "head"),
        P("dp", "ctx", "head"),
        P("dp", "head", "ctx"),
        P("dp", "head", "ctx"),
        P("dp", "ctx", "head"),
        P("dp", "ctx", "head"),
        P("dp", "ctx", "head"),
        P(),
    )
    out_specs = (P("dp", "ctx", "head"), P("dp", "ctx", "head"), P("head", ("ctx", "dp"), None))
    return jax.shard_map(
        functools.partial(on_device, nctx, nhead // NYH),
        mesh=mesh, in_specs=in_specs, out_specs=out_specs, check_vma=False,
    )
```

time: 91.3 us -> 79.6 us (0.87)
  local copies, waits for them, and re-layouts: 8.57 us -> 1.5 us
  Pallas kernels: 81.7 us -> 74.8 us
  other arithmetic: 0 us -> 2.39 us
    unnamed x19 -> x6, local copies, waits for them, and re-layouts: 8.57 us -> 1.5 us
    pallas_call x1, Pallas kernels: 81.7 us -> 74.8 us  [on_device(): pl.pallas_call(functools.partial(kernel, nctx, nx), out_shape=(jax.ShapeD...]
    broadcast_in_dim x0 -> x1, other arithmetic: none -> 2.39 us  [on_device(): (outs[0] * (1.0 / math.sqrt(dh)))[None]]
where the time goes in v2:
time: 79.6 us; the launch traced here: 79.3 us
  Pallas kernels  74.8 us (94%)
  other arithmetic  2.39 us (3%)
  local copies, waits for them, and re-layouts  1.5 us (2%)
    pallas_call x1, Pallas kernels, on_device(): pl.pallas_call(functools.partial(kernel, nctx, nx), out_shape=(jax.ShapeD...  74.8 us
    broadcast_in_dim x1, other arithmetic, on_device(): (outs[0] * (1.0 / math.sqrt(dh)))[None]  2.39 us

profile of v2, /device:TPU:1, one launch (start us, length us, event | category | flops | bytes accessed | tf_op | source)
XLA Modules:
  0.0 79.3 jit_solution(9678901109224053255)
XLA Ops:
  0.6 74.8 %shard_map.103 = (f32[256,1024]{1,0:T(8,128)}, f32[256,256]{1,0:T(8,128)}, f32[8,2048]{1,0:T(8,128)}) custom-call(s32[64]{0:T(128)} %slots.1, bf16[256,1024]{1,0:T(8,128)(2,1)} %bitcast.13, bf16[256,1024]{1,0:T(8,128)(2,1)} %bitcast.14, f32[8,256]{1,0:T(8,128)} %bitcast.18, f32[8,256]{1,0:T(8,128)} %bitcast.19, bf16[256,256]{1,0:T(8,128)(2,1)} %bitcast.17, ...), custom_call_target="tpu_custom_call" | custom-call | flops 2000000000 | bytes 6000000 | tf_op jit(solution)/shard_map/pallas_call | solution.py:343
  75.4 0.0 copy-start
  75.4 2.4 %multiply_bitcast_fusion = f32[1,256,1024]{2,1,0:T(8,128)} fusion(f32[256,1024]{1,0:T(8,128)} %get-tuple-element.6), kind=kLoop, calls=%fused_computation | loop fusion | flops 262144 | bytes 2097152 | tf_op jit(solution)/shard_map/broadcast_in_dim | solution.py:390
  77.8 0.0 copy-done
  77.8 0.0 copy-start.1
  77.8 0.7 copy.13
  78.5 0.2 copy-done.1
  78.7 0.6 copy.14
Async XLA Ops:
  75.4 2.4 %copy-start = (f32[256,256]{1,0:T(8,128)S(1)}, f32[256,256]{1,0:T(8,128)}, u32[]{:S(2)}) copy-start(f32[256,256]{1,0:T(8,128)} %get-tuple-element.7) | copy-start | bytes 786436
  77.8 0.9 %copy-start.1 = (f32[8,2048]{1,0:T(8,128)S(1)}, f32[8,2048]{1,0:T(8,128)}, u32[]{:S(2)}) copy-start(f32[8,2048]{1,0:T(8,128)} %get-tuple-element.8) | copy-start | bytes 196612

commit v3 on v2

--- a/solution.py
+++ b/solution.py
@@ -99,60 +99,9 @@
             for p_ in (0, 1):
                 greet(at(e_=e_, y_=mine, p_=p_))
 
-    pl.semaphore_wait(barrier, 6 + len(group) + NYH - 1)
-
-    sends = []
-    for part, buf in ((0, kb), (1, vb)):
-        cols = slice(part * dh, (part + 1) * dh)
-        for side, to in ((0, right), (1, left)):
-            sends.append(send(kv.at[:, cols], buf.at[side], s_kv.at[part, side], r_kv.at[part, side], dev(c=to)))
-
     fetched[0].wait()
     lt[x, e, p] = feats[...].T
-    own = lt.at[x, e, p]
-    hf = F // 2
-    passed = []
-
-    def pass_on(ref, sem, to):
-        passed.append(send(ref, ref, s_l.at[len(passed)], sem, to))
-
-    to_core = at(p_=1 - p)
-    pass_on(own, r_l.at[0], at(e_=1 - e))
-    if nx > 1:
-        xp, xm, xo = xs[1], xs[nx - 1], xs[2]
-        pass_on(own, r_l.at[1], at(x_=xp))
-        pass_on(own, r_l.at[3], at(x_=xm))
-    pass_on(own, r_core.at[0, 0], to_core)
-
-    def share_other():
-        other = lt.at[x, 1 - e, p]
-        arrived(other, r_l.at[0])
-        if nx > 1:
-            pass_on(other, r_l.at[2], at(x_=xp))
-            pass_on(other, r_l.at[4], at(x_=xm))
-        pass_on(other, r_core.at[0, 1], to_core)
-
-    def share_side(a):
-        if nx > 1:
-            e_ = 1 - e if a else e
-            low, high = lt.at[xm, e_, p], lt.at[xp, e_, p]
-            arrived(low, r_l.at[1 + a])
-            pass_on(low.at[:hf], r_l.at[5 + a], at(x_=xp))
-            arrived(high, r_l.at[3 + a])
-            pass_on(high.at[hf:], r_l.at[7 + a], at(x_=xm))
-            pass_on(low, r_core.at[nx - 1, a], to_core)
-            pass_on(high, r_core.at[1, a], to_core)
-
-    def share_far(a):
-        if nx > 1:
-            far = lt.at[xo, 1 - e if a else e, p]
-            arrived(far.at[:hf], r_l.at[5 + a])
-            arrived(far.at[hf:], r_l.at[7 + a])
-            pass_on(far, r_core.at[2, a], to_core)
-
-    for copy in fetched[1:4]:
-        copy.wait()
-
+    fetched[1].wait()
     for side, blk in ((0, left), (1, right)):
         for kh in (0, 1):
             for qh in (0, 1):
@@ -160,6 +109,71 @@
                 lanes = slice(qh * half, (qh + 1) * half)
                 lrow[side, kh, :, lanes] = lse[:, lanes] * LOG2E + hidden
 
+    pl.semaphore_wait(barrier, 6 + len(group) + NYH - 1)
+
+    sends = []
+    for part, buf in ((0, kb), (1, vb)):
+        cols = slice(part * dh, (part + 1) * dh)
+        for side, to in ((0, right), (1, left)):
+            sends.append(send(kv.at[:, cols], buf.at[side], s_kv.at[part, side], r_kv.at[part, side], dev(c=to)))
+
+    own = lt.at[x, e, p]
+    hf = F // 2
+    passed = []
+
+    def pass_on(ref, sem, to):
+        passed.append(send(ref, ref, s_l.at[len(passed)], sem, to))
+
+    halves = (slice(0, hf), slice(hf, F))
+    to_core, to_e = at(p_=1 - p), at(e_=1 - e)
+    if nx > 1:
+        xp, xm, xo = xs[1], xs[nx - 1], xs[2]
+        to_xp, to_xm = at(x_=xp), at(x_=xm)
+    for h in (0, 1):
+        pass_on(own.at[halves[h]], r_l.at[0, h], to_e)
+        if nx > 1:
+            pass_on(own.at[halves[h]], r_l.at[1, h], to_xp)
+            pass_on(own.at[halves[1 - h]], r_l.at[3, 1 - h], to_xm)
+    pass_on(own, r_core.at[0, 0], to_core)
+
+    def share_other():
+        other = lt.at[x, 1 - e, p]
+        for h in (0, 1):
+            arrived(other.at[halves[h]], r_l.at[0, h])
+            if nx > 1:
+                pass_on(other.at[halves[h]], r_l.at[2, h], to_xp)
+                pass_on(other.at[halves[h]], r_l.at[4, h], to_xm)
+        pass_on(other, r_core.at[0, 1], to_core)
+
+    def near_pair(a):
+        e_ = 1 - e if a else e
+        return lt.at[xm, e_, p], lt.at[xp, e_, p]
+
+    def share_side(a):
+        if nx > 1:
+            low, high = near_pair(a)
+            arrived(low.at[halves[0]], r_l.at[1 + a, 0])
+            pass_on(low.at[halves[0]], r_l.at[5 + a, 0], to_xp)
+            arrived(high.at[halves[1]], r_l.at[3 + a, 1])
+            pass_on(high.at[halves[1]], r_l.at[7 + a, 1], to_xm)
+
+    def share_near(a):
+        if nx > 1:
+            low, high = near_pair(a)
+            arrived(low.at[halves[1]], r_l.at[1 + a, 1])
+            pass_on(low, r_core.at[nx - 1, a], to_core)
+            arrived(high.at[halves[0]], r_l.at[3 + a, 0])
+            pass_on(high, r_core.at[1, a], to_core)
+
+    def share_far(a):
+        if nx > 1:
+            far = lt.at[xo, 1 - e if a else e, p]
+            arrived(far.at[halves[0]], r_l.at[5 + a, 0])
+            arrived(far.at[halves[1]], r_l.at[7 + a, 1])
+            pass_on(far, r_core.at[2, a], to_core)
+
+    for copy in fetched[2:4]:
+        copy.wait()
     heads = [slice(m * dh, (m + 1) * dh) for m in range(hq)]
     for side, to in ((0, left), (1, right)):
         arrived(kb.at[side], r_kv.at[0, side])
@@ -175,6 +189,7 @@
         sends.append(send(dv.at[side], rdv.at[side], s_part.at[0, side], r_part.at[0, side], dev(c=to)))
 
     share_other()
+    share_side(0)
 
     for copy in fetched[4:]:
         copy.wait()
@@ -191,12 +206,12 @@
             totals[side] = term if totals[side] is None else totals[side] + term
             term = tn(ds, kb[side])
             whole = term if whole is None else whole + term
-        qg[:, lanes] = whole
+        qg[:, lanes] = whole * scale
     for side, to in ((0, left), (1, right)):
         dk[side] = totals[side] * scale
         sends.append(send(dk.at[side], rdk.at[side], s_part.at[1, side], r_part.at[1, side], dev(c=to)))
 
-    share_side(0)
+    share_near(0)
 
     for side in (0, 1):
         arrived(rdv.at[side], r_part.at[0, side])
@@ -215,12 +230,15 @@
     def _():
         send(vgb, vall.at[e, p], s_v.at[0], r_v.at[e, p], at(e_=te, p_=tp))
 
+    share_side(1)
     share_far(0)
-    share_side(1)
+    share_near(1)
 
     for side in (0, 1):
         arrived(rdk.at[side], r_part.at[1, side])
     kvg[:, :dh] = kvin[:, :dh] + rdk[0] + rdk[1]
+
+    share_far(1)
 
     for e_ in (0, 1):
         for p_ in (0, 1):
@@ -275,8 +293,6 @@
     beside = (at(z_=(z + 1) % nz), at(z_=(z + nz - 1) % nz))
     beyond = (at(z_=(z + 2) % nz), at(z_=(z + nz - 2) % nz))
     for g in range(ng):
-        if per == 2 and g == 1:
-            share_far(1)
         for i in range(g * per, (g + 1) * per):
             weight_term(i)
         stop(0, g, 0)
@@ -326,6 +342,24 @@
             src_ref=vgb, dst_ref=vall.at[e, p], send_sem=s_v.at[0], recv_sem=r_v.at[e, p],
             device_id=at(e_=te, p_=tp), device_id_type=MESH,
         ).wait_send()
+
+
+def hand_over(a, b, c, a_out, b_out, c_out, a_here, b_here, c_here, sems):
+    n = a.shape[0] // 4
+    cuts = [slice(i * n, (i + 1) * n) for i in range(4)]
+    moves = [(a.at[cut], a_here.at[cut], a_out.at[cut]) for cut in cuts]
+    moves += [(b, b_here, b_out), (c, c_here, c_out)]
+    steps = [
+        (pltpu.make_async_copy(src, here, sems.at[0, i]), pltpu.make_async_copy(here, dst, sems.at[1, i]))
+        for i, (src, here, dst) in enumerate(moves)
+    ]
+    for take, _ in steps:
+        take.start()
+    for take, give in steps:
+        take.wait()
+        give.start()
+    for _, give in steps:
+        give.wait()
 
 
 def on_device(nctx, nx, query, out_grad, row_lse, row_delta, key_value, kv_grad_in, layer_input, slot_order):
@@ -375,7 +409,7 @@
             pltpu.VMEM((NYH * nx, rows, dh), f32),
             pltpu.VMEM((2, 2, hq, S), f32),
             dma((6,)), dma((2, 2)), dma((2, 2)), dma((2, 2)), dma((2, 2)),
-            dma((20,)), dma((9,)), dma((nx, 2)),
+            dma((32,)), dma((9, 2)), dma((nx, 2)),
             dma((4,)), dma((2, 2)),
             dma((2, kc, ng)), dma((2, kc, ng)), dma((2, kc, ng)), dma((2, kc, ng)),
             dma((16,)), dma((nx, 2, 2)),
@@ -387,7 +421,15 @@
     )(
         slot_order, query[0], out_grad[0], row_lse[0], row_delta[0], key_value[0], kv_grad_in[0], layer_input[0]
     )
-    return (outs[0] * (1.0 / math.sqrt(dh)))[None], outs[1][None], outs[2][None]
+    outs = pl.pallas_call(
+        hand_over,
+        out_shape=tuple(jax.ShapeDtypeStruct(o.shape, o.dtype) for o in outs),
+        in_specs=[pl.BlockSpec(memory_space=pl.ANY)] * 3,
+        out_specs=(pl.BlockSpec(memory_space=pl.ANY),) * 3,
+        scratch_shapes=[pltpu.VMEM(o.shape, o.dtype) for o in outs] + [dma((2, 6))],
+        compiler_params=pltpu.CompilerParams(vmem_limit_bytes=58 * 1024 * 1024),
+    )(*outs)
+    return outs[0][None], outs[1][None], outs[2][None]
 
 
 def solution(mesh):

time: 79.6 us -> 77 us (0.967)
  other arithmetic: 2.39 us -> 0 us
  local copies, waits for them, and re-layouts: 1.5 us -> 0 us
  Pallas kernels: 74.8 us -> 76.2 us
    broadcast_in_dim x1 -> x0, other arithmetic: 2.39 us -> none  [on_device(): (outs[0] * (1.0 / math.sqrt(dh)))[None]]
    pallas_call x0 -> x1, Pallas kernels: none -> 2.12 us  [on_device(): pl.pallas_call(hand_over, out_shape=tuple((jax.ShapeDtypeStruct(o.shape,...]
    unnamed x6 -> x0, local copies, waits for them, and re-layouts: 1.5 us -> none
where the time goes in v3:
time: 77 us; the launch traced here: 76.8 us
  Pallas kernels  76.2 us (99%)
    pallas_call x1, Pallas kernels, on_device(): pl.pallas_call(functools.partial(kernel, nctx, nx), out_shape=(jax.ShapeD...  74.1 us
    pallas_call x1, Pallas kernels, on_device(): pl.pallas_call(hand_over, out_shape=tuple((jax.ShapeDtypeStruct(o.shape,...  2.12 us

profile of v3, /device:TPU:1, one launch (start us, length us, event | category | flops | bytes accessed | tf_op | source)
XLA Modules:
  0.0 76.8 jit_solution(7480753043638280623)
XLA Ops:
  0.6 74.1 %shard_map.103 = (f32[256,1024]{1,0:T(8,128)}, f32[256,256]{1,0:T(8,128)}, f32[8,2048]{1,0:T(8,128)}) custom-call(s32[64]{0:T(128)} %slots.1, bf16[256,1024]{1,0:T(8,128)(2,1)} %bitcast.11, bf16[256,1024]{1,0:T(8,128)(2,1)} %bitcast.12, f32[8,256]{1,0:T(8,128)} %bitcast.18, f32[8,256]{1,0:T(8,128)} %bitcast.19, bf16[256,256]{1,0:T(8,128)(2,1)} %bitcast.16, ...), custom_call_target="tpu_custom_call" | custom-call | flops 2000000000 | bytes 6000000 | tf_op jit(solution)/shard_map/pallas_call | solution.py:377
  74.7 2.1 %shard_map.104 = (f32[256,1024]{1,0:T(8,128)}, f32[256,256]{1,0:T(8,128)}, f32[8,2048]{1,0:T(8,128)}) custom-call(f32[256,1024]{1,0:T(8,128)} %get-tuple-element.9.a, f32[256,256]{1,0:T(8,128)} %get-tuple-element.10.b, f32[8,2048]{1,0:T(8,128)} %get-tuple-element.11.c), custom_call_target="tpu_custom_call" | custom-call | tf_op jit(solution)/shard_map/pallas_call | solution.py:424

commit v4 on v3

--- a/solution.py
+++ b/solution.py
@@ -219,7 +219,7 @@
     kvg[:, dh:] = new_v
     vgb[...] = new_v.astype(jnp.bfloat16)
     te, tp = yh // 2, yh % 2
-    for o in range(1, NYH):
+    for o in (2, 1, 3):
         sends.append(send(vgb, vall.at[e, p], s_v.at[o], r_v.at[e, p], at(e_=te, y_=(yh + o) % NYH, p_=tp)))
 
     @pl.when(mine == yh)
@@ -296,15 +296,20 @@
         for i in range(g * per, (g + 1) * per):
             weight_term(i)
         stop(0, g, 0)
-        for i in range(kc):
-            next_odd(i, g, 1)
-            next_odd(i, g, 0)
+        next_odd(0, g, 1)
+        next_odd(0, g, 0)
     for i in range(kc):
+        if i + 1 < kc:
+            for g in range(ng):
+                next_odd(i + 1, g, 1)
         for g in range(ng):
             if i > 0:
                 stop(i, g, 0)
             if i < kc - 1:
                 stop(i, g, 1)
+        if i + 1 < kc:
+            for g in range(ng):
+                next_odd(i + 1, g, 0)
 
     for i, r in enumerate(order):
         g, k = i // per, i % per

time: 77 us -> 77.2 us (level)
  no operation moved by 1% of the time
where the time goes in v4:
time: 77.2 us; the launch traced here: 77 us
  Pallas kernels  76.4 us (99%)
    pallas_call x1, Pallas kernels, on_device(): pl.pallas_call(functools.partial(kernel, nctx, nx), out_shape=(jax.ShapeD...  74.2 us
    pallas_call x1, Pallas kernels, on_device(): pl.pallas_call(hand_over, out_shape=tuple((jax.ShapeDtypeStruct(o.shape,...  2.12 us

profile of v4, /device:TPU:1, one launch (start us, length us, event | category | flops | bytes accessed | tf_op | source)
XLA Modules:
  0.0 77.0 jit_solution(7886981156910974553)
XLA Ops:
  0.6 74.2 %shard_map.103 = (f32[256,1024]{1,0:T(8,128)}, f32[256,256]{1,0:T(8,128)}, f32[8,2048]{1,0:T(8,128)}) custom-call(s32[64]{0:T(128)} %slots.1, bf16[256,1024]{1,0:T(8,128)(2,1)} %bitcast.11, bf16[256,1024]{1,0:T(8,128)(2,1)} %bitcast.12, f32[8,256]{1,0:T(8,128)} %bitcast.18, f32[8,256]{1,0:T(8,128)} %bitcast.19, bf16[256,256]{1,0:T(8,128)(2,1)} %bitcast.16, ...), custom_call_target="tpu_custom_call" | custom-call | flops 2000000000 | bytes 6000000 | tf_op jit(solution)/shard_map/pallas_call | solution.py:382
  74.9 2.1 %shard_map.104 = (f32[256,1024]{1,0:T(8,128)}, f32[256,256]{1,0:T(8,128)}, f32[8,2048]{1,0:T(8,128)}) custom-call(f32[256,1024]{1,0:T(8,128)} %get-tuple-element.9.a, f32[256,256]{1,0:T(8,128)} %get-tuple-element.10.b, f32[8,2048]{1,0:T(8,128)} %get-tuple-element.11.c), custom_call_target="tpu_custom_call" | custom-call | tf_op jit(solution)/shard_map/pallas_call | solution.py:429

commit v5 on v4

--- a/solution.py
+++ b/solution.py
@@ -234,10 +234,6 @@
     share_far(0)
     share_near(1)
 
-    for side in (0, 1):
-        arrived(rdk.at[side], r_part.at[1, side])
-    kvg[:, :dh] = kvin[:, :dh] + rdk[0] + rdk[1]
-
     share_far(1)
 
     for e_ in (0, 1):
@@ -310,6 +306,10 @@
         if i + 1 < kc:
             for g in range(ng):
                 next_odd(i + 1, g, 0)
+
+    for side in (0, 1):
+        arrived(rdk.at[side], r_part.at[1, side])
+    kvg[:, :dh] = kvin[:, :dh] + rdk[0] + rdk[1]
 
     for i, r in enumerate(order):
         g, k = i // per, i % per

time: 77.2 us -> 77.2 us (level)
  no operation moved by 1% of the time
where the time goes in v5:
time: 77.2 us; the launch traced here: 77 us
  Pallas kernels  76.4 us (99%)
    pallas_call x1, Pallas kernels, on_device(): pl.pallas_call(functools.partial(kernel, nctx, nx), out_shape=(jax.ShapeD...  74.2 us
    pallas_call x1, Pallas kernels, on_device(): pl.pallas_call(hand_over, out_shape=tuple((jax.ShapeDtypeStruct(o.shape,...  2.12 us

profile of v5, /device:TPU:1, one launch (start us, length us, event | category | flops | bytes accessed | tf_op | source)
XLA Modules:
  0.0 77.0 jit_solution(11453882874553356246)
XLA Ops:
  0.6 74.2 %shard_map.103 = (f32[256,1024]{1,0:T(8,128)}, f32[256,256]{1,0:T(8,128)}, f32[8,2048]{1,0:T(8,128)}) custom-call(s32[64]{0:T(128)} %slots.1, bf16[256,1024]{1,0:T(8,128)(2,1)} %bitcast.11, bf16[256,1024]{1,0:T(8,128)(2,1)} %bitcast.12, f32[8,256]{1,0:T(8,128)} %bitcast.18, f32[8,256]{1,0:T(8,128)} %bitcast.19, bf16[256,256]{1,0:T(8,128)(2,1)} %bitcast.16, ...), custom_call_target="tpu_custom_call" | custom-call | flops 2000000000 | bytes 6000000 | tf_op jit(solution)/shard_map/pallas_call | solution.py:382
  74.9 2.1 %shard_map.104 = (f32[256,1024]{1,0:T(8,128)}, f32[256,256]{1,0:T(8,128)}, f32[8,2048]{1,0:T(8,128)}) custom-call(f32[256,1024]{1,0:T(8,128)} %get-tuple-element.9.a, f32[256,256]{1,0:T(8,128)} %get-tuple-element.10.b, f32[8,2048]{1,0:T(8,128)} %get-tuple-element.11.c), custom_call_target="tpu_custom_call" | custom-call | tf_op jit(solution)/shard_map/pallas_call | solution.py:429
